TPU v7x, 32 devices: a whole 2x2x4 slice. The times are simulated.
32 devices in a mesh: dp: 8 (over z, x), tensor: 4 (over y, core).
Axes of the slice: x: 2, y: 2, z: 4, core: 2. Of those that a mesh axis runs over, the one named last changes fastest.
Arguments:
- tokens: bfloat16 [32768, 256], P('dp'), may hold values from -6 to 6
- positions: bfloat16 [32768, 256], P('dp'), may hold values from -1 to 1
- segment_ids: int32 [8, 4096], P('dp'), may hold values from 0 to 4, as said below
- pad_flags: int32 [8, 4096], P('dp'), may hold values from 0 to 1, as said below
- cotangent: bfloat16 [32768, 256], P('dp'), may hold values from -6 to 6
- inward: float32 [3, 256, 256], P(None, 'dp', 'tensor'), may hold values from -0.375 to 0.375
- outward: float32 [256, 256], P('tensor', 'dp'), may hold values from -1 to 1
- upward: float32 [256, 2048], P('dp', 'tensor'), may hold values from -0.375 to 0.375
- downward: float32 [2048, 256], P('tensor', 'dp'), may hold values from -0.1875 to 0.1875
- vectors: float32 [6, 256], P(None, 'dp')
- offsets: float32 [2, 256], P(None, ('tensor', 'dp')), may hold values from -4 to 4
- shifts: float32 [2048], P(('tensor', 'dp')), may hold values from -4 to 4
- first_inward: float32 [3, 256, 256], P(None, 'dp', 'tensor'), may hold values from -1536 to 1536
- first_outward: float32 [256, 256], P('tensor', 'dp'), may hold values from -224 to 224
- first_upward: float32 [256, 2048], P('dp', 'tensor'), may hold values from -224 to 224
- first_downward: float32 [2048, 256], P('tensor', 'dp'), may hold values from -512 to 512
- first_vectors: float32 [6, 256], P(None, 'dp'), may hold values from -768 to 768
- first_offsets: float32 [2, 256], P(None, ('tensor', 'dp')), may hold values from -1536 to 1536
- first_shifts: float32 [2048], P(('tensor', 'dp')), may hold values from -224 to 224
- second_inward: float32 [3, 256, 256], P(None, 'dp', 'tensor'), may hold values from 73728 to 294912
- second_outward: float32 [256, 256], P('tensor', 'dp'), may hold values from 1310.72 to 5242.88
- second_upward: float32 [256, 2048], P('dp', 'tensor'), may hold values from 1310.72 to 5242.88
- second_downward: float32 [2048, 256], P('tensor', 'dp'), may hold values from 6553.6 to 26214.4
- second_vectors: float32 [6, 256], P(None, 'dp'), may hold values from 16384 to 65536
- second_offsets: float32 [2, 256], P(None, ('tensor', 'dp')), may hold values from 73728 to 294912
- second_shifts: float32 [2048], P(('tensor', 'dp')), may hold values from 1310.72 to 5242.88
Outputs:
- encoded: bfloat16 [32768, 256], P('dp')
- token_grad: float32 [32768, 256], P('dp')
- grad_inward: float32 [3, 256, 256], P(None, 'dp', 'tensor')
- grad_outward: float32 [256, 256], P('tensor', 'dp')
- grad_upward: float32 [256, 2048], P('dp', 'tensor')
- grad_downward: float32 [2048, 256], P('tensor', 'dp')
- grad_vectors: float32 [6, 256], P(None, 'dp')
- grad_offsets: float32 [2, 256], P(None, ('tensor', 'dp'))
- grad_shifts: float32 [2048], P(('tensor', 'dp'))
- updated_inward: float32 [3, 256, 256], P(None, 'dp', 'tensor')
- updated_outward: float32 [256, 256], P('tensor', 'dp')
- updated_upward: float32 [256, 2048], P('dp', 'tensor')
- updated_downward: float32 [2048, 256], P('tensor', 'dp')
- updated_vectors: float32 [6, 256], P(None, 'dp')
- updated_offsets: float32 [2, 256], P(None, ('tensor', 'dp'))
- updated_shifts: float32 [2048], P(('tensor', 'dp'))
- lowered_inward: bfloat16 [3, 256, 256], P(None, 'dp', 'tensor')
- lowered_outward: bfloat16 [256, 256], P('tensor', 'dp')
- lowered_upward: bfloat16 [256, 2048], P('dp', 'tensor')
- lowered_downward: bfloat16 [2048, 256], P('tensor', 'dp')
- momentum_inward: float32 [3, 256, 256], P(None, 'dp', 'tensor')
- momentum_outward: float32 [256, 256], P('tensor', 'dp')
- momentum_upward: float32 [256, 2048], P('dp', 'tensor')
- momentum_downward: float32 [2048, 256], P('tensor', 'dp')
- momentum_vectors: float32 [6, 256], P(None, 'dp')
- momentum_offsets: float32 [2, 256], P(None, ('tensor', 'dp'))
- momentum_shifts: float32 [2048], P(('tensor', 'dp'))
- variance_inward: float32 [3, 256, 256], P(None, 'dp', 'tensor')
- variance_outward: float32 [256, 256], P('tensor', 'dp')
- variance_upward: float32 [256, 2048], P('dp', 'tensor')
- variance_downward: float32 [2048, 256], P('tensor', 'dp')
- variance_vectors: float32 [6, 256], P(None, 'dp')
- variance_offsets: float32 [2, 256], P(None, ('tensor', 'dp'))
- variance_shifts: float32 [2048], P(('tensor', 'dp'))
Inputs may be any that keep to these rules, and one draw needn't show every extreme that they name: `segment_ids`: in every pack the ids never fall and every id from 0 to 4 occurs. `pad_flags`: the first token of every image is never padding.
All inputs are finite; a program needn't handle non-finite values.
Results may differ from a plain program's by a relative error of at most 0.008.
The roundings to bfloat16 on the way count: a program that leaves them out, or rounds other values in their place, can miss the bound.
Values may be sent and summed in bfloat16 or wider, within the bound.
A program may use at most 128 MiB of HBM per device.

v0:
```python
import jax
import jax.numpy as jnp
from jax import lax
from jax.sharding import PartitionSpec as P

HEAD_DIM = 32
STEP = 10


neg_fill = -1e30
norm_eps = 1e-05
beta_one = 0.5
beta_two = 0.5
adam_eps = 1e-08
decay_rate = 0.0001
step_rates = (0.06, 0.15, 0.06, 0.03, 0.1, 0.1, 0.1)
block_limit = 512


def product(left_side, right_side):
    return jnp.dot(left_side, right_side, preferred_element_type=jnp.float32)


def product_left(left_side, right_side):
    return lax.dot_general(
        left_side, right_side, (((0,), (0,)), ((), ())), preferred_element_type=jnp.float32
    )


def product_right(left_side, right_side):
    return lax.dot_general(
        left_side, right_side, (((1,), (1,)), ((), ())), preferred_element_type=jnp.float32
    )


def smooth_unit(values):
    return jax.nn.gelu(values, approximate=False)


def norm_forward(values, gain_row, shift_row):
    center = values - jnp.mean(values, axis=-1, keepdims=True)
    inverse = lax.rsqrt(jnp.mean(center * center, axis=-1, keepdims=True) + norm_eps)
    scaled = center * inverse
    return (scaled * gain_row + shift_row, scaled, inverse)


def norm_backward(upstream, scaled, inverse, gain_row):
    spread = upstream * gain_row
    centred = (
        spread
        - jnp.mean(spread, axis=-1, keepdims=True)
        - scaled * jnp.mean(spread * scaled, axis=-1, keepdims=True)
    )
    return (inverse * centred, jnp.sum(upstream * scaled, axis=0), jnp.sum(upstream, axis=0))


def summed(partial_value):
    return lax.psum(partial_value, "tensor")


def mask_scores(query_block, key_heads, seg_block, segment, key_open):
    scores = jnp.einsum(
        "qhd,khd->hqk", query_block, key_heads, preferred_element_type=jnp.float32
    ) * HEAD_DIM ** (-0.5)
    allowed = (seg_block[:, None] == segment[None, :]) & key_open[None, :]
    return jnp.where(allowed[None], scores, neg_fill)


def attend_forward(queries, key_rows, values, segment, key_open):
    row_count = queries.shape[0]
    block_rows = min(block_limit, row_count)
    heads_here = queries.shape[1] // HEAD_DIM
    key_heads = key_rows.reshape(row_count, heads_here, HEAD_DIM)
    value_heads = values.reshape(row_count, heads_here, HEAD_DIM)

    def one_block(block_index):
        first_row = block_index * block_rows
        query_block = lax.dynamic_slice_in_dim(queries, first_row, block_rows, 0).reshape(
            block_rows, heads_here, HEAD_DIM
        )
        seg_block = lax.dynamic_slice_in_dim(segment, first_row, block_rows, 0)
        scores = mask_scores(query_block, key_heads, seg_block, segment, key_open)
        maxima = jnp.max(scores, axis=-1, keepdims=True)
        exponent = jnp.exp(scores - maxima)
        totals = jnp.sum(exponent, axis=-1, keepdims=True)
        weights = (exponent / totals).astype(jnp.bfloat16)
        context = jnp.einsum(
            "hqk,khd->qhd", weights, value_heads, preferred_element_type=jnp.float32
        )
        return (
            context.reshape(block_rows, heads_here * HEAD_DIM),
            (maxima + jnp.log(totals))[:, :, 0],
        )

    contexts, log_totals = lax.map(one_block, jnp.arange(row_count // block_rows))
    return (contexts.reshape(row_count, heads_here * HEAD_DIM), log_totals)


def attend_backward(queries, key_rows, values, segment, key_open, log_totals, context_grad):
    row_count = queries.shape[0]
    block_rows = min(block_limit, row_count)
    heads_here = queries.shape[1] // HEAD_DIM
    key_heads = key_rows.reshape(row_count, heads_here, HEAD_DIM)
    value_heads = values.reshape(row_count, heads_here, HEAD_DIM)
    scale_value = HEAD_DIM ** (-0.5)

    def one_block(carry, block_index):
        key_total, value_total = carry
        first_row = block_index * block_rows
        query_block = lax.dynamic_slice_in_dim(queries, first_row, block_rows, 0).reshape(
            block_rows, heads_here, HEAD_DIM
        )
        grad_block = lax.dynamic_slice_in_dim(context_grad, first_row, block_rows, 0).reshape(
            block_rows, heads_here, HEAD_DIM
        )
        seg_block = lax.dynamic_slice_in_dim(segment, first_row, block_rows, 0)
        scores = mask_scores(query_block, key_heads, seg_block, segment, key_open)
        probs = jnp.exp(scores - log_totals[block_index][:, :, None])
        prob_grad = jnp.einsum(
            "qhd,khd->hqk", grad_block, value_heads, preferred_element_type=jnp.float32
        )
        delta = jnp.sum(probs * prob_grad, axis=-1, keepdims=True)
        score_grad = (probs * (prob_grad - delta)).astype(jnp.bfloat16)
        query_grad = (
            jnp.einsum("hqk,khd->qhd", score_grad, key_heads, preferred_element_type=jnp.float32)
            * scale_value
        )
        key_total = key_total + jnp.einsum(
            "hqk,qhd->khd", score_grad, query_block, preferred_element_type=jnp.float32
        )
        value_total = value_total + jnp.einsum(
            "hqk,qhd->khd",
            probs.astype(jnp.bfloat16),
            grad_block,
            preferred_element_type=jnp.float32,
        )
        return (
            (key_total, value_total),
            query_grad.astype(jnp.bfloat16).reshape(block_rows, heads_here * HEAD_DIM),
        )

    zeros_init = jnp.zeros((row_count, heads_here, HEAD_DIM), jnp.float32)
    (key_total, value_total), query_grads = lax.scan(
        one_block, (zeros_init, zeros_init), jnp.arange(row_count // block_rows)
    )
    query_grad = query_grads.reshape(row_count, heads_here * HEAD_DIM)
    key_grad = (
        (key_total * scale_value).astype(jnp.bfloat16).reshape(row_count, heads_here * HEAD_DIM)
    )
    value_grad = value_total.astype(jnp.bfloat16).reshape(row_count, heads_here * HEAD_DIM)
    return (query_grad, key_grad, value_grad)


def adamw(master, gradient, old_first, old_second, step_rate):
    momentum = beta_one * old_first + (1.0 - beta_one) * gradient
    variance = beta_two * old_second + (1.0 - beta_two) * gradient * gradient
    normal_step = (
        momentum / (1.0 - beta_one**STEP) / (jnp.sqrt(variance / (1.0 - beta_two**STEP)) + adam_eps)
    )
    return (master - step_rate * (normal_step + decay_rate * master), momentum, variance)


def body(
    tokens,
    positions,
    segment_ids,
    pad_flags,
    cotangent,
    inward,
    outward,
    upward,
    downward,
    vectors,
    offsets,
    shifts,
    first_inward,
    first_outward,
    first_upward,
    first_downward,
    first_vectors,
    first_offsets,
    first_shifts,
    second_inward,
    second_outward,
    second_upward,
    second_downward,
    second_vectors,
    second_offsets,
    second_shifts,
):
    w_inward, w_outward, w_upward, w_downward, vector_low, offset_low, shift_low = (
        lax.all_gather(inward.astype(jnp.bfloat16), "dp", axis=1, tiled=True),
        lax.all_gather(outward.astype(jnp.bfloat16), "dp", axis=1, tiled=True),
        lax.all_gather(upward.astype(jnp.bfloat16), "dp", axis=0, tiled=True),
        lax.all_gather(downward.astype(jnp.bfloat16), "dp", axis=1, tiled=True),
        lax.all_gather(vectors.astype(jnp.bfloat16), "dp", axis=1, tiled=True),
        lax.all_gather(offsets.astype(jnp.bfloat16), "dp", axis=1, tiled=True),
        lax.all_gather(shifts.astype(jnp.bfloat16), "dp", axis=0, tiled=True),
    )
    vector_wide = vector_low.astype(jnp.float32)
    offset_wide = offset_low.astype(jnp.float32)
    shift_wide = shift_low.astype(jnp.float32)
    segment = segment_ids[0]
    key_open = pad_flags[0] == 0
    input_wide = tokens.astype(jnp.float32)
    query_in = (input_wide + positions.astype(jnp.float32)).astype(jnp.bfloat16)
    queries = (product(query_in, w_inward[0]) + offset_wide[0]).astype(jnp.bfloat16)
    key_rows = product(query_in, w_inward[1]).astype(jnp.bfloat16)
    values = (product(tokens, w_inward[2]) + offset_wide[1]).astype(jnp.bfloat16)
    context, log_totals = attend_forward(queries, key_rows, values, segment, key_open)
    context_low = context.astype(jnp.bfloat16)
    first_sum = input_wide + summed(product(context_low, w_outward)) + vector_wide[4]
    normed, scaled_one, inverse_one = norm_forward(first_sum, vector_wide[0], vector_wide[1])
    normed_low = normed.astype(jnp.bfloat16)
    hidden = product(normed_low, w_upward) + shift_wide
    unit_value, unit_back = jax.vjp(smooth_unit, hidden)
    active = unit_value.astype(jnp.bfloat16)
    second_sum = normed + summed(product(active, w_downward)) + vector_wide[5]
    result, scaled_two, inverse_two = norm_forward(second_sum, vector_wide[2], vector_wide[3])
    encoded = result.astype(jnp.bfloat16)
    upstream = cotangent.astype(jnp.float32)
    second_grad, gain_two, shift_two = norm_backward(
        upstream, scaled_two, inverse_two, vector_wide[2]
    )
    down_low = second_grad.astype(jnp.bfloat16)
    grad_downward = product_left(active, down_low)
    hidden_low = unit_back(product_right(down_low, w_downward))[0].astype(jnp.bfloat16)
    grad_upward = product_left(normed_low, hidden_low)
    grad_shifts = jnp.sum(hidden_low.astype(jnp.float32), axis=0)
    normed_grad = second_grad + summed(product_right(hidden_low, w_upward))
    first_grad, gain_one, shift_one = norm_backward(
        normed_grad, scaled_one, inverse_one, vector_wide[0]
    )
    first_low = first_grad.astype(jnp.bfloat16)
    grad_outward = product_left(context_low, first_low)
    context_grad = product_right(first_low, w_outward).astype(jnp.bfloat16)
    query_grad, key_grad, value_grad = attend_backward(
        queries, key_rows, values, segment, key_open, log_totals, context_grad
    )
    grad_inward = jnp.stack(
        [
            product_left(query_in, query_grad),
            product_left(query_in, key_grad),
            product_left(tokens, value_grad),
        ]
    )
    grad_offsets = jnp.stack(
        [
            jnp.sum(query_grad.astype(jnp.float32), axis=0),
            jnp.sum(value_grad.astype(jnp.float32), axis=0),
        ]
    )
    input_part = (
        product_right(query_grad, w_inward[0])
        + product_right(key_grad, w_inward[1])
        + product_right(value_grad, w_inward[2])
    )
    input_grad = first_grad + summed(input_part)
    grad_vectors = jnp.stack(
        [
            gain_one,
            shift_one,
            gain_two,
            shift_two,
            jnp.sum(first_grad, axis=0),
            jnp.sum(second_grad, axis=0),
        ]
    )
    reduced = (
        lax.psum_scatter(grad_inward, "dp", scatter_dimension=1, tiled=True),
        lax.psum_scatter(grad_outward, "dp", scatter_dimension=1, tiled=True),
        lax.psum_scatter(grad_upward, "dp", scatter_dimension=0, tiled=True),
        lax.psum_scatter(grad_downward, "dp", scatter_dimension=1, tiled=True),
        lax.psum_scatter(grad_vectors, "dp", scatter_dimension=1, tiled=True),
        lax.psum_scatter(grad_offsets, "dp", scatter_dimension=1, tiled=True),
        lax.psum_scatter(grad_shifts, "dp", scatter_dimension=0, tiled=True),
    )
    masters = (inward, outward, upward, downward, vectors, offsets, shifts)
    firsts = (
        first_inward,
        first_outward,
        first_upward,
        first_downward,
        first_vectors,
        first_offsets,
        first_shifts,
    )
    seconds = (
        second_inward,
        second_outward,
        second_upward,
        second_downward,
        second_vectors,
        second_offsets,
        second_shifts,
    )
    updated = []
    momenta = []
    variances = []
    for master, gradient, old_first, old_second, step_rate in zip(
        masters, reduced, firsts, seconds, step_rates
    ):
        new_master, momentum, variance = adamw(master, gradient, old_first, old_second, step_rate)
        updated.append(new_master)
        momenta.append(momentum)
        variances.append(variance)
    return (
        encoded,
        input_grad,
        reduced[0],
        reduced[1],
        reduced[2],
        reduced[3],
        reduced[4],
        reduced[5],
        reduced[6],
        updated[0],
        updated[1],
        updated[2],
        updated[3],
        updated[4],
        updated[5],
        updated[6],
        updated[0].astype(jnp.bfloat16),
        updated[1].astype(jnp.bfloat16),
        updated[2].astype(jnp.bfloat16),
        updated[3].astype(jnp.bfloat16),
        momenta[0],
        momenta[1],
        momenta[2],
        momenta[3],
        momenta[4],
        momenta[5],
        momenta[6],
        variances[0],
        variances[1],
        variances[2],
        variances[3],
        variances[4],
        variances[5],
        variances[6],
    )


def solution(mesh):
    in_specs = (
        P("dp", None),
        P("dp", None),
        P("dp", None),
        P("dp", None),
        P("dp", None),
        P(None, "dp", "tensor"),
        P("tensor", "dp"),
        P("dp", "tensor"),
        P("tensor", "dp"),
        P(None, "dp"),
        P(None, ("tensor", "dp")),
        P(("tensor", "dp")),
        P(None, "dp", "tensor"),
        P("tensor", "dp"),
        P("dp", "tensor"),
        P("tensor", "dp"),
        P(None, "dp"),
        P(None, ("tensor", "dp")),
        P(("tensor", "dp")),
        P(None, "dp", "tensor"),
        P("tensor", "dp"),
        P("dp", "tensor"),
        P("tensor", "dp"),
        P(None, "dp"),
        P(None, ("tensor", "dp")),
        P(("tensor", "dp")),
    )
    out_specs = (
        P("dp", None),
        P("dp", None),
        P(None, "dp", "tensor"),
        P("tensor", "dp"),
        P("dp", "tensor"),
        P("tensor", "dp"),
        P(None, "dp"),
        P(None, ("tensor", "dp")),
        P(("tensor", "dp")),
        P(None, "dp", "tensor"),
        P("tensor", "dp"),
        P("dp", "tensor"),
        P("tensor", "dp"),
        P(None, "dp"),
        P(None, ("tensor", "dp")),
        P(("tensor", "dp")),
        P(None, "dp", "tensor"),
        P("tensor", "dp"),
        P("dp", "tensor"),
        P("tensor", "dp"),
        P(None, "dp", "tensor"),
        P("tensor", "dp"),
        P("dp", "tensor"),
        P("tensor", "dp"),
        P(None, "dp"),
        P(None, ("tensor", "dp")),
        P(("tensor", "dp")),
        P(None, "dp", "tensor"),
        P("tensor", "dp"),
        P("dp", "tensor"),
        P("tensor", "dp"),
        P(None, "dp"),
        P(None, ("tensor", "dp")),
        P(("tensor", "dp")),
    )
    return jax.shard_map(body, mesh=mesh, in_specs=in_specs, out_specs=out_specs, check_vma=False)
```

profile of v0, /device:TPU:0, one launch (start us, length us, event | category | flops | bytes accessed | tf_op | source)
XLA Modules:
  0.0 1405.5 jit_solution(3010460021737112204)
XLA Ops:
  8.1 22.1 %all-gather = bf16[8,8,2]{1,2,0:T(2,128)(2,1)S(1)} all-gather(bf16[1,8,2]{1,2,0:T(2,128)(2,1)S(1)} %convert_bitcast_fusion.2), channel_id=1, replica_groups=mesh['dp'=8,'tensor'=4] {'dp'}, dimensions={0}, use_global_device_ids=true | all-gather | bytes 288 | tf_op jit(solution)/shard_map/all_gather | solution.py:197
  32.6 32.5 %all_gather.23 = bf16[64,256]{0,1:T(8,128)(2,1)} all-gather(bf16[64,32]{0,1:T(8,128)(2,1)S(1)} %convert_element_type.133), channel_id=1, replica_groups=mesh['dp'=8,'tensor'=4] {'dp'}, dimensions={1}, use_global_device_ids=true | all-gather | bytes 36864 | tf_op jit(solution)/shard_map/all_gather | solution.py:193
  65.1 30.6 %all_gather.21 = bf16[3,256,64]{2,1,0:T(8,128)(2,1)S(1)} all-gather(bf16[3,32,64]{2,1,0:T(8,128)(2,1)S(1)} %convert_element_type.125), channel_id=1, replica_groups=mesh['dp'=8,'tensor'=4] {'dp'}, dimensions={1}, use_global_device_ids=true | all-gather | bytes 110592 | tf_op jit(solution)/shard_map/all_gather | solution.py:192
  101.7 152.2 %while.27 = (s32[]{:T(128)}, bf16[8,512,64]{1,2,0:T(8,128)(2,1)S(1)}, f32[8,2,512]{2,1,0:T(2,128)}, s32[8]{0:T(128)S(1)}, s32[4096]{0:T(1024)}, /*index=5*/s32[1...) while((s32[]{:T(128)}, ...), condition=%wide.region_3.4_spmd, body=%wide.region_0.3_spmd.sunk | while | flops 591395840 | bytes 60221656 | solution.py:95
  259.9 17.6 %all-reduce = bf16[512]{0:T(512)(128)(2,1)S(1)} all-reduce(bf16[512]{0:T(512)(128)(2,1)S(1)} %dynamic-update-slice), channel_id=1, replica_groups=mesh['dp'=8,'tensor'=4] {'dp'}, use_global_device_ids=true, to_apply=%add | all-reduce | flops 512 | bytes 2048
  277.6 26.0 %all-gather.1 = bf16[8,32,6]{1,2,0:T(8,128)(2,1)S(1)} all-gather(bf16[1,32,6]{1,2,0:T(8,128)(2,1)S(1)} %convert_bitcast_fusion.1), channel_id=1, replica_groups=mesh['dp'=8,'tensor'=4] {'dp'}, dimensions={0}, use_global_device_ids=true | all-gather | bytes 3456 | tf_op jit(solution)/shard_map/all_gather | solution.py:196
  303.7 30.9 %all_gather.27 = bf16[512,256]{0,1:T(8,128)(2,1)S(1)} all-gather(bf16[512,32]{0,1:T(8,128)(2,1)S(1)} %convert_element_type.141), channel_id=1, replica_groups=mesh['dp'=8,'tensor'=4] {'dp'}, dimensions={1}, use_global_device_ids=true | all-gather | bytes 294912 | tf_op jit(solution)/shard_map/all_gather | solution.py:195
  334.6 30.7 %all_gather.25 = bf16[256,512]{1,0:T(8,128)(2,1)S(1)} all-gather(bf16[32,512]{1,0:T(8,128)(2,1)S(1)} %convert_element_type.137), channel_id=1, replica_groups=mesh['dp'=8,'tensor'=4] {'dp'}, dimensions={0}, use_global_device_ids=true | all-gather | bytes 294912 | tf_op jit(solution)/shard_map/all_gather | solution.py:194
  371.8 21.6 %multiply_convert_fusion.1 = (bf16[4096,512]{1,0:T(8,128)(2,1)S(1)}, f32[4096,512]{1,0:T(8,128)}, f32[4096,512]{1,0:T(8,128)}) fusion(f32[512]{0:T(512)S(1)} %convert_element_type.139, bf16[4096,256]{1,0:T(8,128)(2,1)S(1)} %fusion.36, bf16[256,512]{1,0:T(8,128)(2,1)S(1)} %all_gather.25), kind=kOutput, calls=%fused_computation.35 | convolution fusion | flops 1212153856 | bytes 23332864 | tf_op jit(solution)/shard_map/dot_general | solution.py:21
  398.9 82.9 %all-reduce.13.cloned.1.call-done = f32[4096,256]{1,0:T(8,128)} async-done(((f32[4096,256]{1,0:T(8,128)}), f32[4096,256]{1,0:T(8,128)}) %all-reduce.13.cloned.1.call-update) | async-done | bytes 4194320 | tf_op jit(solution)/shard_map/psum | solution.py:58
  521.2 74.9 %all-reduce.15.cloned.1.call-done = f32[4096,256]{1,0:T(8,128)} async-done(((f32[4096,256]{1,0:T(8,128)}), f32[4096,256]{1,0:T(8,128)}) %all-reduce.15.cloned.1.call-update) | async-done | bytes 4194320 | tf_op jit(solution)/shard_map/psum | solution.py:58
  610.2 476.9 %while.28 = (s32[]{:T(128)}, f32[4096,2,32]{0,2,1:T(8,128)S(1)}, f32[4096,2,32]{0,2,1:T(8,128)}, bf16[8,512,64]{1,2,0:T(8,128)(2,1)}, s32[8]{0:T(128)S(1)}, /*in...) while((s32[]{:T(128)}, f32[4096,2,32]{0,2,1:T(8,128)S(1)}, ...), condition=%wide.region_17.18_spmd.clone, body=%wide.region_15.17_spmd.clone.sunk | while | flops 1410399232 | bytes 220977600 | solution.py:143
  637.1 15.4 %multiply_reduce_fusion.7 = (f32[2,512]{1,0:T(2,128)S(1)}, f32[2,512,4096]{2,1,0:T(8,128)}) fusion(f32[2,512,4096]{2,1,0:T(8,128)} %copy-done, f32[2,512]{1,0:T(2,128)S(1)} %dynamic-slice_bitcast_fusion.2, pred[512,4096]{1,0:T(8,128)(4,1)} %compare_and_fusion.5, bf16[512,2,32]{0,2,1:T(8,128)(2,1)} %bitcast.191, ...), kind=kOutput, calls=%fused_computation.13.clone.1 | convolution fusion | flops 289405952 | bytes 36249600 | tf_op jit(solution)/shard_map/while/body/eval_jaxpr/qhd,khd->hqk/dot_general | solution.py:119
  652.5 12.5 multiply_convert_fusion.4
  696.8 15.4 %multiply_reduce_fusion.7 = (f32[2,512]{1,0:T(2,128)S(1)}, f32[2,512,4096]{2,1,0:T(8,128)}) fusion(f32[2,512,4096]{2,1,0:T(8,128)} %copy-done, f32[2,512]{1,0:T(2,128)S(1)} %dynamic-slice_bitcast_fusion.2, pred[512,4096]{1,0:T(8,128)(4,1)} %compare_and_fusion.5, bf16[512,2,32]{0,2,1:T(8,128)(2,1)} %bitcast.191, ...), kind=kOutput, calls=%fused_computation.13.clone.1 | convolution fusion | flops 289405952 | bytes 36249600 | tf_op jit(solution)/shard_map/while/body/eval_jaxpr/qhd,khd->hqk/dot_general | solution.py:119
  712.2 12.5 multiply_convert_fusion.4
  756.4 15.4 %multiply_reduce_fusion.7 = (f32[2,512]{1,0:T(2,128)S(1)}, f32[2,512,4096]{2,1,0:T(8,128)}) fusion(f32[2,512,4096]{2,1,0:T(8,128)} %copy-done, f32[2,512]{1,0:T(2,128)S(1)} %dynamic-slice_bitcast_fusion.2, pred[512,4096]{1,0:T(8,128)(4,1)} %compare_and_fusion.5, bf16[512,2,32]{0,2,1:T(8,128)(2,1)} %bitcast.191, ...), kind=kOutput, calls=%fused_computation.13.clone.1 | convolution fusion | flops 289405952 | bytes 36249600 | tf_op jit(solution)/shard_map/while/body/eval_jaxpr/qhd,khd->hqk/dot_general | solution.py:119
  771.8 12.4 multiply_convert_fusion.4
  816.0 15.4 %multiply_reduce_fusion.7 = (f32[2,512]{1,0:T(2,128)S(1)}, f32[2,512,4096]{2,1,0:T(8,128)}) fusion(f32[2,512,4096]{2,1,0:T(8,128)} %copy-done, f32[2,512]{1,0:T(2,128)S(1)} %dynamic-slice_bitcast_fusion.2, pred[512,4096]{1,0:T(8,128)(4,1)} %compare_and_fusion.5, bf16[512,2,32]{0,2,1:T(8,128)(2,1)} %bitcast.191, ...), kind=kOutput, calls=%fused_computation.13.clone.1 | convolution fusion | flops 289405952 | bytes 36249600 | tf_op jit(solution)/shard_map/while/body/eval_jaxpr/qhd,khd->hqk/dot_general | solution.py:119
  831.4 12.4 multiply_convert_fusion.4
  875.6 15.4 %multiply_reduce_fusion.7 = (f32[2,512]{1,0:T(2,128)S(1)}, f32[2,512,4096]{2,1,0:T(8,128)}) fusion(f32[2,512,4096]{2,1,0:T(8,128)} %copy-done, f32[2,512]{1,0:T(2,128)S(1)} %dynamic-slice_bitcast_fusion.2, pred[512,4096]{1,0:T(8,128)(4,1)} %compare_and_fusion.5, bf16[512,2,32]{0,2,1:T(8,128)(2,1)} %bitcast.191, ...), kind=kOutput, calls=%fused_computation.13.clone.1 | convolution fusion | flops 289405952 | bytes 36249600 | tf_op jit(solution)/shard_map/while/body/eval_jaxpr/qhd,khd->hqk/dot_general | solution.py:119
  891.0 12.4 multiply_convert_fusion.4
  935.2 15.4 %multiply_reduce_fusion.7 = (f32[2,512]{1,0:T(2,128)S(1)}, f32[2,512,4096]{2,1,0:T(8,128)}) fusion(f32[2,512,4096]{2,1,0:T(8,128)} %copy-done, f32[2,512]{1,0:T(2,128)S(1)} %dynamic-slice_bitcast_fusion.2, pred[512,4096]{1,0:T(8,128)(4,1)} %compare_and_fusion.5, bf16[512,2,32]{0,2,1:T(8,128)(2,1)} %bitcast.191, ...), kind=kOutput, calls=%fused_computation.13.clone.1 | convolution fusion | flops 289405952 | bytes 36249600 | tf_op jit(solution)/shard_map/while/body/eval_jaxpr/qhd,khd->hqk/dot_general | solution.py:119
  950.6 12.4 multiply_convert_fusion.4
  994.7 15.4 %multiply_reduce_fusion.7 = (f32[2,512]{1,0:T(2,128)S(1)}, f32[2,512,4096]{2,1,0:T(8,128)}) fusion(f32[2,512,4096]{2,1,0:T(8,128)} %copy-done, f32[2,512]{1,0:T(2,128)S(1)} %dynamic-slice_bitcast_fusion.2, pred[512,4096]{1,0:T(8,128)(4,1)} %compare_and_fusion.5, bf16[512,2,32]{0,2,1:T(8,128)(2,1)} %bitcast.191, ...), kind=kOutput, calls=%fused_computation.13.clone.1 | convolution fusion | flops 289405952 | bytes 36249600 | tf_op jit(solution)/shard_map/while/body/eval_jaxpr/qhd,khd->hqk/dot_general | solution.py:119
  1010.1 12.4 multiply_convert_fusion.4
  1054.3 15.4 %multiply_reduce_fusion.7 = (f32[2,512]{1,0:T(2,128)S(1)}, f32[2,512,4096]{2,1,0:T(8,128)}) fusion(f32[2,512,4096]{2,1,0:T(8,128)} %copy-done, f32[2,512]{1,0:T(2,128)S(1)} %dynamic-slice_bitcast_fusion.2, pred[512,4096]{1,0:T(8,128)(4,1)} %compare_and_fusion.5, bf16[512,2,32]{0,2,1:T(8,128)(2,1)} %bitcast.191, ...), kind=kOutput, calls=%fused_computation.13.clone.1 | convolution fusion | flops 289405952 | bytes 36249600 | tf_op jit(solution)/shard_map/while/body/eval_jaxpr/qhd,khd->hqk/dot_general | solution.py:119
  1120.0 21.4 %all-reduce.4 = (f32[2,64]{1,0:T(2,128)S(1)}, f32[512]{0:T(512)S(1)}) all-reduce(f32[2,64]{1,0:T(2,128)S(1)} %pad_maximum_fusion.1, f32[512]{0:T(512)S(1)} %copy-done.57), channel_id=7, replica_groups=mesh['dp'=8,'tensor'=4] {'dp'}, use_global_device_ids=true, to_apply=%region_32.33.clone | all-reduce | flops 640 | bytes 5120
  1142.6 23.5 %reduce-scatter.14.cloned.1.call-done = f32[32,6]{1,0:T(8,128)} async-done(((f32[256,6]{1,0:T(8,128)}), f32[32,6]{1,0:T(8,128)}) %reduce-scatter.14.cloned.1.call-update) | async-done | bytes 784
  1167.6 62.7 %reduce-scatter.8.cloned.1.call-done = f32[64,32]{0,1:T(8,128)} async-done(((f32[64,256]{0,1:T(8,128)}), f32[64,32]{0,1:T(8,128)}) %reduce-scatter.8.cloned.1.call-update) | async-done | bytes 8208 | tf_op jit(solution)/shard_map/reduce_scatter | solution.py:271
  1231.7 73.9 %all-reduce.19.cloned.1.call-done = f32[3,256,64]{2,0,1:T(4,128)} async-done(((f32[3,256,64]{2,0,1:T(4,128)}), f32[3,256,64]{2,0,1:T(4,128)}) %all-reduce.19.cloned.1.call-update) | async-done | bytes 196624
  1307.1 85.6 %all-reduce.17.cloned.1.call-done = f32[4096,256]{1,0:T(8,128)} async-done(((f32[4096,256]{1,0:T(8,128)}), f32[4096,256]{1,0:T(8,128)}) %all-reduce.17.cloned.1.call-update) | async-done | bytes 4194320 | tf_op jit(solution)/shard_map/psum | solution.py:58
  (473 shorter events, 513.7 us)
Async XLA Ops:
  7.2 91.4 %copy-start.12 = (bf16[4096,256]{1,0:T(8,128)(2,1)S(1)}, bf16[4096,256]{1,0:T(8,128)(2,1)}, u32[]{:S(2)}) copy-start(bf16[4096,256]{1,0:T(8,128)(2,1)} %param.30) | copy-start | bytes 6291460
  7.2 358.1 %all-reduce.11.cloned.1.call-start = ((), (), s32[]{:S(2)}) async-start(), calls=%async_computation.4 | async-start | bytes 8388608 | tf_op jit(solution)/shard_map/psum | solution.py:58
  101.7 153.8 %copy-start.29 = (bf16[64,256]{0,1:T(8,128)(2,1)S(1)}, bf16[64,256]{0,1:T(8,128)(2,1)}, u32[]{:S(2)}) copy-start(bf16[64,256]{0,1:T(8,128)(2,1)} %all_gather.23) | copy-start | bytes 98308
  255.5 22.1 %copy-start.46 = (f32[6,32]{1,0:T(8,128)S(1)}, f32[6,32]{1,0:T(8,128)}, u32[]{:S(2)}) copy-start(f32[6,32]{1,0:T(8,128)} %param.39) | copy-start | bytes 2308
  255.5 48.2 %copy-start.33 = (f32[32,512]{1,0:T(8,128)S(1)}, f32[32,512]{1,0:T(8,128)}, u32[]{:S(2)}) copy-start(f32[32,512]{1,0:T(8,128)} %param.37) | copy-start | bytes 196612
  255.5 48.2 %copy-start.31 = (f32[512,32]{0,1:T(8,128)S(1)}, f32[512,32]{0,1:T(8,128)}, u32[]{:S(2)}) copy-start(f32[512,32]{0,1:T(8,128)} %param.38) | copy-start | bytes 196612
  255.5 109.8 %copy-start.13 = (bf16[4096,256]{1,0:T(8,128)(2,1)S(1)}, bf16[4096,256]{1,0:T(8,128)(2,1)}, u32[]{:S(2)}) copy-start(bf16[4096,256]{1,0:T(8,128)(2,1)} %param.30) | copy-start | bytes 6291460
  258.3 223.4 %all-reduce.13.cloned.1.call-start = ((), (), s32[]{:S(2)}) async-start(), calls=%async_computation.5 | async-start | bytes 8388608 | tf_op jit(solution)/shard_map/psum | solution.py:58
  371.8 21.6 %copy-start.24 = (bf16[4096,256]{1,0:T(8,128)(2,1)}, bf16[4096,256]{1,0:T(8,128)(2,1)S(1)}, u32[]{:S(2)}) copy-start(bf16[4096,256]{1,0:T(8,128)(2,1)S(1)} %fusion.36) | copy-start | bytes 6291460
  398.8 197.3 %all-reduce.15.cloned.1.call-start = ((), (), s32[]{:S(2)}) async-start(), calls=%async_computation.6 | async-start | bytes 8388608 | tf_op jit(solution)/shard_map/psum | solution.py:58
  510.3 606.2 %reduce-scatter.12.cloned.1.call-start = ((), (), s32[]{:S(2)}) async-start(), calls=%async_computation.10 | async-start | bytes 589824 | tf_op jit(solution)/shard_map/reduce_scatter | solution.py:273
  516.0 602.2 %reduce-scatter.10.cloned.1.call-start = ((), (), s32[]{:S(2)}) async-start(), calls=%async_computation.9 | async-start | bytes 589824 | tf_op jit(solution)/shard_map/reduce_scatter | solution.py:272
  521.2 645.0 %reduce-scatter.14.cloned.1.call-start = ((), (), s32[]{:S(2)}) async-start(), calls=%async_computation.11 | async-start | bytes 147456
  1105.0 125.3 %reduce-scatter.8.cloned.1.call-start = ((), (), s32[]{:S(2)}) async-start(), calls=%async_computation.8 | async-start | bytes 147456 | tf_op jit(solution)/shard_map/reduce_scatter | solution.py:271
  1105.8 199.8 %all-reduce.19.cloned.1.call-start = ((), (), s32[]{:S(2)}) async-start(), calls=%async_computation.12 | async-start | bytes 1048576
  1109.1 283.6 %all-reduce.17.cloned.1.call-start = ((), (), s32[]{:S(2)}) async-start(), calls=%async_computation.7 | async-start | bytes 8388608 | tf_op jit(solution)/shard_map/psum | solution.py:58
  1114.2 27.2 %copy-start.62 = (f32[64]{0:T(128)S(1)}, f32[64]{0:T(128)}, u32[]{:S(2)}) copy-start(f32[64]{0:T(128)} %param.41) | copy-start | bytes 772
  1114.2 27.2 %copy-start.63 = (f32[64]{0:T(128)S(1)}, f32[64]{0:T(128)}, u32[]{:S(2)}) copy-start(f32[64]{0:T(128)} %param.48) | copy-start | bytes 772
  1114.2 27.1 %copy-start.64 = (f32[64]{0:T(128)S(1)}, f32[64]{0:T(128)}, u32[]{:S(2)}) copy-start(f32[64]{0:T(128)} %param.55) | copy-start | bytes 772
  1114.2 27.8 %copy-start.58 = (f32[2,8]{1,0:T(2,128)S(1)}, f32[2,8]{1,0:T(2,128)}, u32[]{:S(2)}) copy-start(f32[2,8]{1,0:T(2,128)} %param.40) | copy-start | bytes 196
  1114.2 27.7 %copy-start.59 = (f32[2,8]{1,0:T(2,128)S(1)}, f32[2,8]{1,0:T(2,128)}, u32[]{:S(2)}) copy-start(f32[2,8]{1,0:T(2,128)} %param.47) | copy-start | bytes 196
  1114.2 27.7 %copy-start.60 = (f32[2,8]{1,0:T(2,128)S(1)}, f32[2,8]{1,0:T(2,128)}, u32[]{:S(2)}) copy-start(f32[2,8]{1,0:T(2,128)} %param.54) | copy-start | bytes 196
  1114.2 52.7 %copy-start.47 = (f32[6,32]{1,0:T(8,128)S(1)}, f32[6,32]{1,0:T(8,128)}, u32[]{:S(2)}) copy-start(f32[6,32]{1,0:T(8,128)} %param.39) | copy-start | bytes 2308
  1114.3 52.7 %copy-start.53 = (f32[6,32]{1,0:T(8,128)S(1)}, f32[6,32]{1,0:T(8,128)}, u32[]{:S(2)}) copy-start(f32[6,32]{1,0:T(8,128)} %param.46) | copy-start | bytes 2308
  1114.3 52.7 %copy-start.54 = (f32[6,32]{1,0:T(8,128)S(1)}, f32[6,32]{1,0:T(8,128)}, u32[]{:S(2)}) copy-start(f32[6,32]{1,0:T(8,128)} %param.53) | copy-start | bytes 2308
  1114.3 116.0 %copy-start.40 = (f32[64,32]{0,1:T(8,128)S(1)}, f32[64,32]{0,1:T(8,128)}, u32[]{:S(2)}) copy-start(f32[64,32]{0,1:T(8,128)} %param.36) | copy-start | bytes 24580
  1114.3 116.0 %copy-start.43 = (f32[64,32]{0,1:T(8,128)S(1)}, f32[64,32]{0,1:T(8,128)}, u32[]{:S(2)}) copy-start(f32[64,32]{0,1:T(8,128)} %param.43) | copy-start | bytes 24580
  1114.3 116.0 %copy-start.44 = (f32[64,32]{0,1:T(8,128)S(1)}, f32[64,32]{0,1:T(8,128)}, u32[]{:S(2)}) copy-start(f32[64,32]{0,1:T(8,128)} %param.50) | copy-start | bytes 24580
  1114.3 192.1 %copy-start.35 = (f32[3,32,64]{2,1,0:T(8,128)S(1)}, f32[3,32,64]{2,1,0:T(8,128)}, u32[]{:S(2)}) copy-start(f32[3,32,64]{2,1,0:T(8,128)} %param.35) | copy-start | bytes 73732
  1114.3 192.1 %copy-start.41 = (f32[3,32,64]{2,1,0:T(8,128)S(1)}, f32[3,32,64]{2,1,0:T(8,128)}, u32[]{:S(2)}) copy-start(f32[3,32,64]{2,1,0:T(8,128)} %param.42) | copy-start | bytes 73732
  1114.3 192.1 %copy-start.42 = (f32[3,32,64]{2,1,0:T(8,128)S(1)}, f32[3,32,64]{2,1,0:T(8,128)}, u32[]{:S(2)}) copy-start(f32[3,32,64]{2,1,0:T(8,128)} %param.49) | copy-start | bytes 73732
  1167.0 231.8 %copy-start.45 = (f32[6,32]{1,0:T(8,128)}, f32[6,32]{1,0:T(8,128)S(1)}, u32[]{:S(2)}) copy-start(f32[6,32]{1,0:T(8,128)S(1)} %copy.106) | copy-start | bytes 2308
  (86 other events, 546.1 us)
Sparse Core Ops, SparseCore 0:
  258.4 82.8 all-reduce.10
  398.9 82.7 all-reduce.12
  510.5 85.6 all-reduce.14
  600.3 61.9 reduce-scatter.11
  666.0 60.9 reduce-scatter.9
  1105.1 60.9 reduce-scatter.13
  1170.4 59.8 reduce-scatter.7
  1234.1 71.4 all-reduce.18
  1307.9 84.7 all-reduce.16
where the time goes:
time: 1420 us; the launch traced here: 1410 us
  waiting for transfers between devices  404 us (28%)
  matrix products  392 us (28%)
  other arithmetic  240 us (17%)
  blocking collectives  212 us (15%)
  local copies, waits for them, and re-layouts  113 us (8%)
  loops' own time  27.1 us (2%)
  between operations  17.7 us (1%)
    psum x4, waiting for transfers between devices, summed(): return lax.psum(partial_value, 'tensor')  243 us
    dot_general x8, matrix products, one_block(): jnp.einsum('qhd,khd->hqk', grad_block, value_heads, preferred_element_typ...  123 us
    convert_element_type x8, other arithmetic, one_block(): score_grad = (probs * (prob_grad - delta)).astype(jnp.bfloat16)  99.3 us
    unnamed x11, waiting for transfers between devices  97.8 us
    dot_general x8, matrix products, one_block(): jnp.einsum('hqk,qhd->khd', probs.astype(jnp.bfloat16), grad_block, prefer...  63.3 us
    reduce_scatter x1, waiting for transfers between devices, body(): lax.psum_scatter(grad_outward, 'dp', scatter_dimension=1, tiled=True)  62.7 us
    dot_general x16, matrix products, mask_scores(): jnp.einsum('qhd,khd->hqk', query_block, key_heads, preferred_element_type...  58.9 us
    and x16, other arithmetic, mask_scores(): allowed = (seg_block[:, None] == segment[None, :]) & key_open[None, :]  46.6 us
  transfers between devices with their start and end apart: 9, of which 6 were waited for; matrix products, arithmetic and copies ran while one was open for 33% of the time, Pallas kernels for 0%

commit v1 on v0

--- a/solution.py
+++ b/solution.py
@@ -1,9 +1,412 @@
+import functools
 import jax
 import jax.numpy as jnp
 from jax import lax
+from jax.experimental import pallas as pl
+from jax.experimental.pallas import tpu as pltpu
 from jax.sharding import PartitionSpec as P
 
 HEAD_DIM = 32
+PACK_ROWS = 4096
+IMAGES = 5
+QUERY_ROWS = 512
+KEY_ROWS = 512
+SPAN = PACK_ROWS + 512
+LOG_SCALE = HEAD_DIM**-0.5 * 1.4426950408889634
+FENCE = 2.0**100
+LARGE = 2.0**100
+SMALL = 2.0**-60
+NN = (((1,), (0,)), ((), ()))
+NT = (((1,), (1,)), ((), ()))
+TN = (((0,), (0,)), ((), ()))
+bf16 = jnp.bfloat16
+f32 = jnp.float32
+
+
+def mm(left, right, dims=NN):
+    return lax.dot_general(left, right, dims, preferred_element_type=f32)
+
+
+def iota(shape, dim):
+    return lax.broadcasted_iota(jnp.int32, shape, dim)
+
+
+def pieces_of(value):
+    one = value.astype(bf16).astype(f32)
+    rest = value - one
+    two = rest.astype(bf16).astype(f32)
+    return one, two, rest - two
+
+
+def attend_forward_kernel(
+    tok, pos, w3, off, seg, pad,
+    packed, ctx, qa, qw, ka, va, rank, bounds,
+    wqd, wkd, compact, dst,
+):
+    lane = iota((256, 128), 1)
+    for which, spread in ((0, wqd), (1, wkd)):
+        base = w3[which].astype(f32)
+        left = pltpu.roll(base, 32, 1)
+        right = pltpu.roll(base, 96, 1)
+        spread[:, :128] = jnp.where(lane < 32, base, jnp.where(lane < 64, left, 0.0)).astype(bf16)
+        spread[:, 128:] = jnp.where(lane < 32, right, jnp.where(lane < 64, base, 0.0)).astype(bf16)
+    lane8 = iota((8, 128), 1)
+    off_rows = off[...]
+    off_left = pltpu.roll(off_rows, 32, 1)
+    off_right = pltpu.roll(off_rows, 96, 1)
+    q_bias = jnp.concatenate(
+        [
+            jnp.where(lane8 < 32, off_rows, jnp.where(lane8 < 64, off_left, 0.0))[0:1],
+            jnp.where(lane8 < 32, off_right, jnp.where(lane8 < 64, off_rows, 0.0))[0:1],
+        ],
+        axis=1,
+    )
+    v_bias = jnp.where(lane8 < 64, off_rows, 0.0)[1:2]
+
+    segment = seg[...]
+    open_key = jnp.where(pad[...] == 0, 1.0, 0.0)
+    grid_row = iota((32, 128), 0)
+    before = (iota((128, 128), 0) < iota((128, 128), 1)).astype(bf16)
+    in_row = mm(open_key.astype(bf16), before)
+    row_total = jnp.broadcast_to(jnp.sum(open_key, axis=1, keepdims=True), (32, 128))
+    above = (iota((32, 32), 1) < iota((32, 32), 0)).astype(bf16)
+    place = (in_row + mm(above, row_total.astype(bf16))).astype(jnp.int32)
+    place = jnp.where(open_key > 0.5, place, -1)
+    for r in range(32):
+        rank[r, :, :] = place[r : r + 1, :]
+    for s in range(IMAGES + 1):
+        if s == 0:
+            bounds[0] = 0
+            bounds[8] = 0
+        else:
+            low = (segment < s).astype(f32)
+            bounds[s] = jnp.sum(low).astype(jnp.int32)
+            bounds[8 + s] = jnp.sum(low * open_key).astype(jnp.int32)
+    for i in range(16):
+        dst[i] = jnp.sum(jnp.where(grid_row < 2 * i, open_key, 0.0)).astype(jnp.int32)
+    for i in range(16):
+        bounds[16 + i] = dst[i]
+    total = bounds[8 + IMAGES]
+
+    lane_row = iota((1, 128), 1)
+    q_from = jnp.full((1, 128), SPAN, jnp.int32)
+    q_to = jnp.full((1, 128), SPAN, jnp.int32)
+    k_from = jnp.full((1, 128), SPAN, jnp.int32)
+    k_to = jnp.full((1, 128), SPAN, jnp.int32)
+    for s in range(IMAGES):
+        at = lane_row == 64 + s
+        q_from = jnp.where(at, bounds[s], q_from)
+        q_to = jnp.where(at, bounds[s + 1], q_to)
+        k_from = jnp.where(at, bounds[8 + s], k_from)
+        k_to = jnp.where(at, bounds[9 + s], k_to)
+
+    compact[pl.ds(0, 16), :] = jnp.zeros((16, 512), bf16)
+    qa[:, pl.ds(PACK_ROWS, SPAN - PACK_ROWS), :] = jnp.zeros((2, SPAN - PACK_ROWS, 128), bf16)
+    qw[pl.ds(PACK_ROWS, SPAN - PACK_ROWS), :] = jnp.zeros((SPAN - PACK_ROWS, 128), bf16)
+
+    lane_q = iota((256, 128), 1)
+    row_q = iota((256, 128), 0)
+
+    def project(i, _):
+        first = pl.multiple_of(i * 256, 256)
+        rows = pl.ds(first, 256)
+        token = tok[rows, :]
+        query_in = (token.astype(f32) + pos[rows, :].astype(f32)).astype(bf16)
+        both = (mm(query_in, wqd[...]) + q_bias).astype(bf16).astype(f32)
+        here = row_q + first
+        outside = (here < q_from) | (here >= q_to)
+        feature = jnp.where(
+            lane_q < 64 + IMAGES, jnp.where(outside, 1.0, 0.0), jnp.where(lane_q == 69, 1.0, 0.0)
+        )
+        for h in range(2):
+            exact = both[:, 128 * h : 128 * h + 128] * LOG_SCALE
+            high = exact.astype(bf16).astype(f32)
+            qa[h, rows, :] = jnp.where(
+                lane_q < 32, high, jnp.where(lane_q < 64, exact - high, feature)
+            ).astype(bf16)
+        qw[rows, :] = jnp.where(
+            lane_q < 32, both[:, :128], jnp.where(lane_q < 64, both[:, 128:], 0.0)
+        ).astype(bf16)
+        start = dst[i]
+        aligned = pl.multiple_of((start // 16) * 16, 16)
+        places = jnp.concatenate([rank[2 * i], rank[2 * i + 1]], axis=1)
+        hot = jnp.where(iota((272, 256), 0) + aligned == places, 1.0, 0.0).astype(bf16)
+        moved = mm(hot, jnp.concatenate([query_in, token], axis=1)).astype(bf16)
+        head = pl.ds(aligned, 16)
+        compact[head, :] = compact[head, :] + moved[:16]
+        compact[pl.ds(pl.multiple_of(aligned + 16, 16), 256), :] = moved[16:]
+        return 0
+
+    lax.fori_loop(0, 16, project, 0)
+
+    lane_k = iota((512, 128), 1)
+    row_k = iota((512, 128), 0)
+
+    def project_keys(i, _):
+        first = pl.multiple_of(i * 512, 512)
+        rows = pl.ds(first, 512)
+        here = row_k + first
+        real = here < total
+        both = mm(compact[rows, 0:256], wkd[...])
+        value = mm(compact[rows, 256:512], w3[2]) + v_bias
+        value = jnp.where(real, value, 0.0)
+        inside = (here >= k_from) & (here < k_to)
+        feature = jnp.where(inside, -FENCE, 0.0)
+        feature = jnp.where(lane_k == 69, jnp.where(real, 0.0, -FENCE), feature)
+        feature = jnp.where((lane_k >= 70) & (lane_k < 73), 1.0, feature)
+        for h in range(2):
+            key = jnp.where(real, both[:, 128 * h : 128 * h + 128], 0.0)
+            ka[h, rows, :] = jnp.where(lane_k < 64, key, feature).astype(bf16)
+        va[0, rows, :] = jnp.where(
+            lane_k < 32, value, jnp.where(lane_k < 35, 1.0, 0.0)
+        ).astype(bf16)
+        va[1, rows, :] = jnp.where(
+            lane_k < 3, 1.0, jnp.where((lane_k >= 32) & (lane_k < 64), value, 0.0)
+        ).astype(bf16)
+        return 0
+
+    lax.fori_loop(0, SPAN // 512, project_keys, 0)
+
+    lane_b = iota((QUERY_ROWS, 128), 1)
+    row_b = iota((QUERY_ROWS, 128), 0)
+
+    def finish(q_rows, q_row, q_start, q_end, sums, shift):
+        at = row_b + q_row
+        mine = (at >= q_start) & (at < q_end)
+        l_zero = jnp.broadcast_to(sums[0][:, 32:33], (QUERY_ROWS, 128))
+        l_one = jnp.broadcast_to(sums[1][:, 0:1], (QUERY_ROWS, 128))
+        joined = jnp.where(
+            lane_b < 32, sums[0] / l_zero, jnp.where(lane_b < 64, sums[1] / l_one, 0.0)
+        )
+        ctx[q_rows, :] = jnp.where(mine, joined, ctx[q_rows, :])
+        for h, total_row in ((0, l_zero), (1, l_one)):
+            one, two, three = pieces_of(-(shift[h] + jnp.log2(total_row)))
+            new = jnp.where(lane_b == 70, one, jnp.where(lane_b == 71, two, three))
+            spot = mine & (lane_b >= 70) & (lane_b < 73)
+            old = qa[h, q_rows, :].astype(f32)
+            qa[h, q_rows, :] = jnp.where(spot, new, old).astype(bf16)
+
+    def per_segment(s, _):
+        q_start, q_end = bounds[s], bounds[s + 1]
+        k_start, k_end = bounds[8 + s], bounds[9 + s]
+        q_first = (q_start // 16) * 16
+        k_first = (k_start // 16) * 16
+        q_steps = (q_end - q_first + QUERY_ROWS - 1) // QUERY_ROWS
+        k_steps = (k_end - k_first + KEY_ROWS - 1) // KEY_ROWS
+
+        def per_query(i, _):
+            q_row = pl.multiple_of(q_first + i * QUERY_ROWS, 16)
+            q_rows = pl.ds(q_row, QUERY_ROWS)
+            zero = jnp.zeros((QUERY_ROWS, 128), f32)
+
+            def per_key(j, sums):
+                k_rows = pl.ds(pl.multiple_of(k_first + j * KEY_ROWS, 16), KEY_ROWS)
+                out = []
+                for h in range(2):
+                    score = mm(qa[h, q_rows, :], ka[h, k_rows, :], NT)
+                    weight = jnp.exp2(score).astype(bf16)
+                    out.append(sums[h] + mm(weight, va[h, k_rows, :]))
+                return tuple(out)
+
+            sums = lax.fori_loop(0, k_steps, per_key, (zero, zero))
+            at = row_b + q_row
+            mine = (at >= q_start) & (at < q_end)
+            check = jnp.where(
+                mine & (lane_b == 32), sums[0], jnp.where(mine & (lane_b == 0), sums[1], 1.0)
+            )
+            fine = (jnp.max(check) < LARGE) & (jnp.min(check) > SMALL)
+
+            @pl.when(fine)
+            def _():
+                finish(q_rows, q_row, q_start, q_end, sums, (0.0, 0.0))
+
+            @pl.when(jnp.logical_not(fine))
+            def _():
+                low = jnp.full((QUERY_ROWS, 128), -3.0e38, f32)
+
+                def peak(j, tops):
+                    k_rows = pl.ds(pl.multiple_of(k_first + j * KEY_ROWS, 16), KEY_ROWS)
+                    out = []
+                    for h in range(2):
+                        score = mm(qa[h, q_rows, :], ka[h, k_rows, :], NT)
+                        out.append(
+                            jnp.maximum(tops[h], jnp.max(score, axis=1, keepdims=True))
+                        )
+                    return tuple(out)
+
+                tops = lax.fori_loop(0, k_steps, peak, (low, low))
+
+                def per_key_safe(j, sums):
+                    k_rows = pl.ds(pl.multiple_of(k_first + j * KEY_ROWS, 16), KEY_ROWS)
+                    out = []
+                    for h in range(2):
+                        score = mm(qa[h, q_rows, :], ka[h, k_rows, :], NT)
+                        weight = jnp.exp2(score - tops[h][:, 0:1]).astype(bf16)
+                        out.append(sums[h] + mm(weight, va[h, k_rows, :]))
+                    return tuple(out)
+
+                safe = lax.fori_loop(0, k_steps, per_key_safe, (zero, zero))
+                finish(q_rows, q_row, q_start, q_end, safe, tops)
+
+            return 0
+
+        lax.fori_loop(0, q_steps, per_query, 0)
+        return 0
+
+    lax.fori_loop(0, IMAGES, per_segment, 0)
+
+    lane_p = iota((512, 128), 1)
+    for t in range(4):
+        upper = ctx[pl.ds(1024 * t, 512), :]
+        lower = pltpu.roll(ctx[pl.ds(1024 * t + 512, 512), :], 64, 1)
+        packed[pl.ds(512 * t, 512), :] = jnp.where(lane_p < 64, upper, lower).astype(bf16)
+
+
+VMEM_SPEC = pl.BlockSpec(memory_space=pltpu.VMEM)
+SMEM_SPEC = pl.BlockSpec(memory_space=pltpu.SMEM)
+
+
+def attend_forward(tokens, positions, w3, off, segment, padding):
+    return pl.pallas_call(
+        attend_forward_kernel,
+        out_shape=(
+            jax.ShapeDtypeStruct((2048, 128), bf16),
+            jax.ShapeDtypeStruct((SPAN, 128), f32),
+            jax.ShapeDtypeStruct((2, SPAN, 128), bf16),
+            jax.ShapeDtypeStruct((SPAN, 128), bf16),
+            jax.ShapeDtypeStruct((2, SPAN, 128), bf16),
+            jax.ShapeDtypeStruct((2, SPAN, 128), bf16),
+            jax.ShapeDtypeStruct((32, 1, 128), jnp.int32),
+            jax.ShapeDtypeStruct((32,), jnp.int32),
+        ),
+        in_specs=[VMEM_SPEC] * 6,
+        out_specs=[VMEM_SPEC] * 7 + [SMEM_SPEC],
+        scratch_shapes=[
+            pltpu.VMEM((256, 256), bf16),
+            pltpu.VMEM((256, 256), bf16),
+            pltpu.VMEM((SPAN, 512), bf16),
+            pltpu.SMEM((16,), jnp.int32),
+        ],
+        compiler_params=pltpu.CompilerParams(vmem_limit_bytes=56 * 2**20),
+        cost_estimate=pl.CostEstimate(
+            flops=20 * 10**9, bytes_accessed=20 * 10**6, transcendentals=10**7
+        ),
+    )(tokens, positions, w3, off, segment.reshape(32, 128), padding.reshape(32, 128))
+
+
+def attend_backward_kernel(
+    packed, ctx, qa, qw, ka, va, rank, bounds, gq, gkv, do, kw, dq, dkv
+):
+    lane = iota((512, 128), 1)
+    for t in range(4):
+        pair = packed[pl.ds(512 * t, 512), :].astype(f32)
+        for half in range(2):
+            rows = pl.ds(1024 * t + 512 * half, 512)
+            grad = pair if half == 0 else pltpu.roll(pair, 64, 1)
+            product = grad * ctx[rows, :]
+            delta_zero = jnp.sum(jnp.where(lane < 32, product, 0.0), axis=1, keepdims=True)
+            delta_one = jnp.sum(
+                jnp.where((lane >= 32) & (lane < 64), product, 0.0), axis=1, keepdims=True
+            )
+            one, two, three = pieces_of(-jnp.broadcast_to(delta_zero, (512, 128)))
+            tail = jnp.where(lane == 32, one, jnp.where(lane == 33, two, three))
+            do[0, rows, :] = jnp.where(
+                lane < 32, grad, jnp.where(lane < 35, tail, 0.0)
+            ).astype(bf16)
+            one, two, three = pieces_of(-jnp.broadcast_to(delta_one, (512, 128)))
+            tail = jnp.where(lane == 0, one, jnp.where(lane == 1, two, three))
+            do[1, rows, :] = jnp.where(
+                lane < 3, tail, jnp.where((lane >= 32) & (lane < 64), grad, 0.0)
+            ).astype(bf16)
+    do[:, pl.ds(PACK_ROWS, SPAN - PACK_ROWS), :] = jnp.zeros((2, SPAN - PACK_ROWS, 128), bf16)
+    for i in range(SPAN // 512):
+        rows = pl.ds(512 * i, 512)
+        dq[rows, :] = jnp.zeros((512, 128), f32)
+        dkv[rows, :] = jnp.zeros((512, 128), f32)
+
+    def per_segment(s, _):
+        q_start, q_end = bounds[s], bounds[s + 1]
+        k_start, k_end = bounds[8 + s], bounds[9 + s]
+        q_first = (q_start // 16) * 16
+        k_first = (k_start // 16) * 16
+        q_steps = (q_end - q_first + QUERY_ROWS - 1) // QUERY_ROWS
+        k_steps = (k_end - k_first + KEY_ROWS - 1) // KEY_ROWS
+
+        def per_key(j, _):
+            k_row = pl.multiple_of(k_first + j * KEY_ROWS, 16)
+            k_rows = pl.ds(k_row, KEY_ROWS)
+            at = iota((KEY_ROWS, 128), 0) + k_row
+            mine = (at >= k_start) & (at < k_end)
+            for h in range(2):
+                mask = mine & (lane >= 32 * h) & (lane < 32 * h + 32)
+                kw[h] = jnp.where(mask, ka[h, k_rows, :].astype(f32), 0.0).astype(bf16)
+
+            def per_query(i, carry):
+                q_rows = pl.ds(pl.multiple_of(q_first + i * QUERY_ROWS, 16), QUERY_ROWS)
+                total = dq[q_rows, :]
+                out = list(carry)
+                for h in range(2):
+                    score = mm(qa[h, q_rows, :], ka[h, k_rows, :], NT)
+                    prob = jnp.exp2(score)
+                    prob_grad = mm(do[h, q_rows, :], va[h, k_rows, :], NT)
+                    score_grad = (prob * prob_grad).astype(bf16)
+                    total = total + mm(score_grad, kw[h])
+                    span = slice(32 * h, 32 * h + 32)
+                    out[h] = out[h] + mm(qw[q_rows, span], score_grad, TN)
+                    out[2 + h] = out[2 + h] + mm(do[h, q_rows, span], prob.astype(bf16), TN)
+                dq[q_rows, :] = total
+                return tuple(out)
+
+            zero = jnp.zeros((32, KEY_ROWS), f32)
+            done = lax.fori_loop(0, q_steps, per_query, (zero,) * 4)
+            fresh = jnp.concatenate(done, axis=0).T
+            dkv[k_rows, :] = dkv[k_rows, :] + jnp.where(mine, fresh, 0.0)
+            return 0
+
+        lax.fori_loop(0, k_steps, per_key, 0)
+        return 0
+
+    lax.fori_loop(0, IMAGES, per_segment, 0)
+
+    lane_t = iota((256, 128), 1)
+
+    def emit(i, _):
+        rows = pl.ds(pl.multiple_of(i * 256, 256), 256)
+        gq[rows, :] = (dq[rows, :] * HEAD_DIM**-0.5).astype(bf16)
+        start = bounds[16 + i]
+        aligned = pl.multiple_of((start // 16) * 16, 16)
+        places = jnp.concatenate([rank[2 * i], rank[2 * i + 1]], axis=1)
+        hot = jnp.where(iota((272, 256), 0) + aligned == places, 1.0, 0.0).astype(bf16)
+        piece = dkv[pl.ds(aligned, 272), :]
+        scale = jnp.where(iota((272, 128), 1) < 64, HEAD_DIM**-0.5, 1.0)
+        gkv[rows, :] = mm(hot, (piece * scale).astype(bf16), TN).astype(bf16)
+        return 0
+
+    lax.fori_loop(0, 16, emit, 0)
+
+
+def attend_backward(packed, ctx, qa, qw, ka, va, rank, bounds):
+    return pl.pallas_call(
+        attend_backward_kernel,
+        out_shape=(
+            jax.ShapeDtypeStruct((PACK_ROWS, 128), bf16),
+            jax.ShapeDtypeStruct((PACK_ROWS, 128), bf16),
+        ),
+        in_specs=[VMEM_SPEC] * 7 + [SMEM_SPEC],
+        out_specs=[VMEM_SPEC] * 2,
+        scratch_shapes=[
+            pltpu.VMEM((2, SPAN, 128), bf16),
+            pltpu.VMEM((2, KEY_ROWS, 128), bf16),
+            pltpu.VMEM((SPAN, 128), f32),
+            pltpu.VMEM((SPAN, 128), f32),
+        ],
+        compiler_params=pltpu.CompilerParams(vmem_limit_bytes=56 * 2**20),
+        cost_estimate=pl.CostEstimate(
+            flops=50 * 10**9, bytes_accessed=20 * 10**6, transcendentals=10**7
+        ),
+    )(packed, ctx, qa, qw, ka, va, rank, bounds)
+
+
 STEP = 10
 
 
@@ -14,7 +417,6 @@
 adam_eps = 1e-08
 decay_rate = 0.0001
 step_rates = (0.06, 0.15, 0.06, 0.03, 0.1, 0.1, 0.1)
-block_limit = 512
 
 
 def product(left_side, right_side):
@@ -56,99 +458,6 @@
 
 def summed(partial_value):
     return lax.psum(partial_value, "tensor")
-
-
-def mask_scores(query_block, key_heads, seg_block, segment, key_open):
-    scores = jnp.einsum(
-        "qhd,khd->hqk", query_block, key_heads, preferred_element_type=jnp.float32
-    ) * HEAD_DIM ** (-0.5)
-    allowed = (seg_block[:, None] == segment[None, :]) & key_open[None, :]
-    return jnp.where(allowed[None], scores, neg_fill)
-
-
-def attend_forward(queries, key_rows, values, segment, key_open):
-    row_count = queries.shape[0]
-    block_rows = min(block_limit, row_count)
-    heads_here = queries.shape[1] // HEAD_DIM
-    key_heads = key_rows.reshape(row_count, heads_here, HEAD_DIM)
-    value_heads = values.reshape(row_count, heads_here, HEAD_DIM)
-
-    def one_block(block_index):
-        first_row = block_index * block_rows
-        query_block = lax.dynamic_slice_in_dim(queries, first_row, block_rows, 0).reshape(
-            block_rows, heads_here, HEAD_DIM
-        )
-        seg_block = lax.dynamic_slice_in_dim(segment, first_row, block_rows, 0)
-        scores = mask_scores(query_block, key_heads, seg_block, segment, key_open)
-        maxima = jnp.max(scores, axis=-1, keepdims=True)
-        exponent = jnp.exp(scores - maxima)
-        totals = jnp.sum(exponent, axis=-1, keepdims=True)
-        weights = (exponent / totals).astype(jnp.bfloat16)
-        context = jnp.einsum(
-            "hqk,khd->qhd", weights, value_heads, preferred_element_type=jnp.float32
-        )
-        return (
-            context.reshape(block_rows, heads_here * HEAD_DIM),
-            (maxima + jnp.log(totals))[:, :, 0],
-        )
-
-    contexts, log_totals = lax.map(one_block, jnp.arange(row_count // block_rows))
-    return (contexts.reshape(row_count, heads_here * HEAD_DIM), log_totals)
-
-
-def attend_backward(queries, key_rows, values, segment, key_open, log_totals, context_grad):
-    row_count = queries.shape[0]
-    block_rows = min(block_limit, row_count)
-    heads_here = queries.shape[1] // HEAD_DIM
-    key_heads = key_rows.reshape(row_count, heads_here, HEAD_DIM)
-    value_heads = values.reshape(row_count, heads_here, HEAD_DIM)
-    scale_value = HEAD_DIM ** (-0.5)
-
-    def one_block(carry, block_index):
-        key_total, value_total = carry
-        first_row = block_index * block_rows
-        query_block = lax.dynamic_slice_in_dim(queries, first_row, block_rows, 0).reshape(
-            block_rows, heads_here, HEAD_DIM
-        )
-        grad_block = lax.dynamic_slice_in_dim(context_grad, first_row, block_rows, 0).reshape(
-            block_rows, heads_here, HEAD_DIM
-        )
-        seg_block = lax.dynamic_slice_in_dim(segment, first_row, block_rows, 0)
-        scores = mask_scores(query_block, key_heads, seg_block, segment, key_open)
-        probs = jnp.exp(scores - log_totals[block_index][:, :, None])
-        prob_grad = jnp.einsum(
-            "qhd,khd->hqk", grad_block, value_heads, preferred_element_type=jnp.float32
-        )
-        delta = jnp.sum(probs * prob_grad, axis=-1, keepdims=True)
-        score_grad = (probs * (prob_grad - delta)).astype(jnp.bfloat16)
-        query_grad = (
-            jnp.einsum("hqk,khd->qhd", score_grad, key_heads, preferred_element_type=jnp.float32)
-            * scale_value
-        )
-        key_total = key_total + jnp.einsum(
-            "hqk,qhd->khd", score_grad, query_block, preferred_element_type=jnp.float32
-        )
-        value_total = value_total + jnp.einsum(
-            "hqk,qhd->khd",
-            probs.astype(jnp.bfloat16),
-            grad_block,
-            preferred_element_type=jnp.float32,
-        )
-        return (
-            (key_total, value_total),
-            query_grad.astype(jnp.bfloat16).reshape(block_rows, heads_here * HEAD_DIM),
-        )
-
-    zeros_init = jnp.zeros((row_count, heads_here, HEAD_DIM), jnp.float32)
-    (key_total, value_total), query_grads = lax.scan(
-        one_block, (zeros_init, zeros_init), jnp.arange(row_count // block_rows)
-    )
-    query_grad = query_grads.reshape(row_count, heads_here * HEAD_DIM)
-    key_grad = (
-        (key_total * scale_value).astype(jnp.bfloat16).reshape(row_count, heads_here * HEAD_DIM)
-    )
-    value_grad = value_total.astype(jnp.bfloat16).reshape(row_count, heads_here * HEAD_DIM)
-    return (query_grad, key_grad, value_grad)
 
 
 def adamw(master, gradient, old_first, old_second, step_rate):
@@ -200,15 +509,15 @@
     vector_wide = vector_low.astype(jnp.float32)
     offset_wide = offset_low.astype(jnp.float32)
     shift_wide = shift_low.astype(jnp.float32)
-    segment = segment_ids[0]
-    key_open = pad_flags[0] == 0
     input_wide = tokens.astype(jnp.float32)
     query_in = (input_wide + positions.astype(jnp.float32)).astype(jnp.bfloat16)
-    queries = (product(query_in, w_inward[0]) + offset_wide[0]).astype(jnp.bfloat16)
-    key_rows = product(query_in, w_inward[1]).astype(jnp.bfloat16)
-    values = (product(tokens, w_inward[2]) + offset_wide[1]).astype(jnp.bfloat16)
-    context, log_totals = attend_forward(queries, key_rows, values, segment, key_open)
-    context_low = context.astype(jnp.bfloat16)
+    w_lanes = jnp.pad(w_inward, ((0, 0), (0, 0), (0, 64)))
+    off_lanes = jnp.pad(offset_wide, ((0, 6), (0, 64)))
+    packed, *saved = attend_forward(
+        tokens, positions, w_lanes, off_lanes, segment_ids, pad_flags
+    )
+    pairs = packed.reshape(4, 512, 2, 64)
+    context_low = pairs.transpose(0, 2, 1, 3).reshape(PACK_ROWS, 64)
     first_sum = input_wide + summed(product(context_low, w_outward)) + vector_wide[4]
     normed, scaled_one, inverse_one = norm_forward(first_sum, vector_wide[0], vector_wide[1])
     normed_low = normed.astype(jnp.bfloat16)
@@ -234,9 +543,11 @@
     first_low = first_grad.astype(jnp.bfloat16)
     grad_outward = product_left(context_low, first_low)
     context_grad = product_right(first_low, w_outward).astype(jnp.bfloat16)
-    query_grad, key_grad, value_grad = attend_backward(
-        queries, key_rows, values, segment, key_open, log_totals, context_grad
-    )
+    halves = context_grad.reshape(4, 2, 512, 64)
+    gq, gkv = attend_backward(
+        halves.transpose(0, 2, 1, 3).reshape(2048, 128), *saved
+    )
+    query_grad, key_grad, value_grad = gq[:, :64], gkv[:, :64], gkv[:, 64:]
     grad_inward = jnp.stack(
         [
             product_left(query_in, query_grad),

time: 1420 us -> 913 us (0.64)
  matrix products: 392 us -> 65.5 us
  other arithmetic: 240 us -> 45.5 us
  local copies, waits for them, and re-layouts: 113 us -> 16.5 us
  Pallas kernels: 0 us -> 75.7 us
  waiting for transfers between devices: 404 us -> 476 us
  loops' own time: 27.1 us -> 0 us
    dot_general x56 -> x0, matrix products: 316 us -> none  [the longest x8 123 us: one_block(): jnp.einsum('qhd,khd->hqk', grad_block, value_heads, preferred_element_typ...]
    convert_element_type x11 -> x0, other arithmetic: 103 us -> none  [the longest x8 99.3 us: one_block(): score_grad = (probs * (prob_grad - delta)).astype(jnp.bfloat16)]
    pallas_call x0 -> x2, Pallas kernels: none -> 75.7 us  [the longest x1 38.9 us: attend_backward(): pl.pallas_call(attend_backward_kernel, out_shape=(jax.ShapeDtypeStruct((P...]
    reduce_scatter x1, waiting for transfers between devices: 0.01 us -> 57.4 us  [body(): lax.psum_scatter(grad_upward, 'dp', scatter_dimension=0, tiled=True)]
    and x16 -> x0, other arithmetic: 46.6 us -> none  [mask_scores(): allowed = (seg_block[:, None] == segment[None, :]) & key_open[None, :]]
    while x96 -> x0, local copies, waits for them, and re-layouts: 46 us -> none
    dynamic_slice x48 -> x0, local copies, waits for them, and re-layouts: 41.1 us -> none  [the longest x16 12.2 us: one_block(): seg_block = lax.dynamic_slice_in_dim(segment, first_row, block_rows, 0)]
    reduce_sum x8 -> x0, other arithmetic: 37.1 us -> none  [one_block(): totals = jnp.sum(exponent, axis=-1, keepdims=True)]
  transfers between devices with their start and end apart: 9 -> 9, of which waited for: 6 -> 7; matrix products, arithmetic and copies ran while one was open for 33% -> 6% of each run, Pallas kernels for 0% -> 4%
where the time goes in v1:
time: 913 us; the launch traced here: 912 us
  waiting for transfers between devices  476 us (52%)
  blocking collectives  215 us (24%)
  Pallas kernels  75.7 us (8%)
  matrix products  65.5 us (7%)
  other arithmetic  45.5 us (5%)
  between operations  17.2 us (2%)
  local copies, waits for them, and re-layouts  16.5 us (2%)
    psum x4, waiting for transfers between devices, summed(): return lax.psum(partial_value, 'tensor')  242 us
    unnamed x11, waiting for transfers between devices  114 us
    reduce_scatter x1, waiting for transfers between devices, body(): lax.psum_scatter(grad_outward, 'dp', scatter_dimension=1, tiled=True)  62.7 us
    reduce_scatter x1, waiting for transfers between devices, body(): lax.psum_scatter(grad_upward, 'dp', scatter_dimension=0, tiled=True)  57.4 us
    unnamed x2, blocking collectives  39.8 us
    pallas_call x1, Pallas kernels, attend_backward(): pl.pallas_call(attend_backward_kernel, out_shape=(jax.ShapeDtypeStruct((P...  38.9 us
    pallas_call x1, Pallas kernels, attend_forward(): pl.pallas_call(attend_forward_kernel, out_shape=(jax.ShapeDtypeStruct((20...  36.9 us
    all_gather x1, blocking collectives, body(): lax.all_gather(outward.astype(jnp.bfloat16), 'dp', axis=1, tiled=True)  34.5 us
  transfers between devices with their start and end apart: 9, of which 7 were waited for; matrix products, arithmetic and copies ran while one was open for 6% of the time, Pallas kernels for 4%

profile of v1, /device:TPU:0, one launch (start us, length us, event | category | flops | bytes accessed | tf_op | source)
XLA Modules:
  0.0 912.0 jit_solution(8696980212741075659)
XLA Ops:
  8.1 32.4 %all_gather.21 = bf16[3,256,64]{2,1,0:T(8,128)(2,1)S(1)} all-gather(bf16[3,32,64]{2,1,0:T(8,128)(2,1)S(1)} %convert_element_type.87), channel_id=1, replica_groups=mesh['dp'=8,'tensor'=4] {'dp'}, dimensions={1}, use_global_device_ids=true | all-gather | bytes 110592 | tf_op jit(solution)/shard_map/all_gather | solution.py:501
  41.2 20.3 %all-gather = bf16[8,8,2]{1,2,0:T(2,128)(2,1)S(1)} all-gather(bf16[1,8,2]{1,2,0:T(2,128)(2,1)S(1)} %convert_bitcast_fusion.1), channel_id=1, replica_groups=mesh['dp'=8,'tensor'=4] {'dp'}, dimensions={0}, use_global_device_ids=true | all-gather | bytes 288 | tf_op jit(solution)/shard_map/all_gather | solution.py:506
  62.9 36.9 %shard_map.513 = (bf16[2048,128]{1,0:T(8,128)(2,1)}, f32[4608,128]{1,0:T(8,128)}, bf16[2,4608,128]{2,1,0:T(8,128)(2,1)}, bf16[4608,128]{1,0:T(8,128)(2,1)}, bf16...) custom-call(bf16[4096,256]{1,0:T(8,128)(2,1)} %tok.1, ...), custom_call_target="tpu_custom_call" | custom-call | flops 20000000000 | bytes 20000000 | tf_op jit(solution)/shard_map/pallas_call | solution.py:270
  102.4 34.5 %all_gather.23 = bf16[64,256]{0,1:T(8,128)(2,1)S(1)} all-gather(bf16[64,32]{0,1:T(8,128)(2,1)S(1)} %convert_element_type.89), channel_id=1, replica_groups=mesh['dp'=8,'tensor'=4] {'dp'}, dimensions={1}, use_global_device_ids=true | all-gather | bytes 36864 | tf_op jit(solution)/shard_map/all_gather | solution.py:502
  137.0 2.8 fusion.58
  139.8 26.0 %all-gather.1 = bf16[8,32,6]{1,2,0:T(8,128)(2,1)S(1)} all-gather(bf16[1,32,6]{1,2,0:T(8,128)(2,1)S(1)} %convert_bitcast_fusion), channel_id=1, replica_groups=mesh['dp'=8,'tensor'=4] {'dp'}, dimensions={0}, use_global_device_ids=true | all-gather | bytes 3456 | tf_op jit(solution)/shard_map/all_gather | solution.py:505
  167.5 20.4 %all-reduce.2 = bf16[512]{0:T(512)(128)(2,1)S(1)} all-reduce(bf16[512]{0:T(512)(128)(2,1)S(1)} %dynamic-update-slice), channel_id=1, replica_groups=mesh['dp'=8,'tensor'=4] {'dp'}, use_global_device_ids=true, to_apply=%add.2 | all-reduce | flops 512 | bytes 2048
  187.9 30.8 %all_gather.25 = bf16[256,512]{1,0:T(8,128)(2,1)S(1)} all-gather(bf16[32,512]{1,0:T(8,128)(2,1)S(1)} %convert_element_type.93), channel_id=1, replica_groups=mesh['dp'=8,'tensor'=4] {'dp'}, dimensions={0}, use_global_device_ids=true | all-gather | bytes 294912 | tf_op jit(solution)/shard_map/all_gather | solution.py:503
  218.6 30.9 %all_gather.27 = bf16[512,256]{0,1:T(8,128)(2,1)S(1)} all-gather(bf16[512,32]{0,1:T(8,128)(2,1)S(1)} %convert_element_type.97), channel_id=1, replica_groups=mesh['dp'=8,'tensor'=4] {'dp'}, dimensions={1}, use_global_device_ids=true | all-gather | bytes 294912 | tf_op jit(solution)/shard_map/all_gather | solution.py:504
  249.6 2.8 fusion.54
  256.1 21.7 %multiply_convert_fusion = (bf16[4096,512]{1,0:T(8,128)(2,1)S(1)}, f32[4096,512]{1,0:T(8,128)}, f32[4096,512]{1,0:T(8,128)}) fusion(f32[512]{0:T(512)S(1)} %convert_element_type.95, bf16[4096,256]{1,0:T(8,128)(2,1)S(1)} %fusion.15, bf16[256,512]{1,0:T(8,128)(2,1)S(1)} %all_gather.25), kind=kOutput, calls=%fused_computation.4 | convolution fusion | flops 1212153856 | bytes 23332864 | tf_op jit(solution)/shard_map/dot_general | solution.py:423
  279.7 3.3 fusion.59
  283.1 82.8 %all-reduce.15.cloned.1.call-done = f32[4096,256]{1,0:T(8,128)} async-done(((f32[4096,256]{1,0:T(8,128)}), f32[4096,256]{1,0:T(8,128)}) %all-reduce.15.cloned.1.call-update) | async-done | bytes 4194320 | tf_op jit(solution)/shard_map/psum | solution.py:460
  365.9 4.4 fusion.52
  374.7 4.9 fusion.49
  379.6 8.0 convert_reduce_fusion
  389.5 3.2 fusion.60
  393.1 5.6 fusion.19
  400.7 4.3 fusion.61
  405.0 73.6 %all-reduce.17.cloned.1.call-done = f32[4096,256]{1,0:T(8,128)} async-done(((f32[4096,256]{1,0:T(8,128)}), f32[4096,256]{1,0:T(8,128)}) %all-reduce.17.cloned.1.call-update) | async-done | bytes 4194320 | tf_op jit(solution)/shard_map/psum | solution.py:460
  478.6 6.1 multiply_reduce_fusion
  484.8 3.2 fusion.51
  493.3 38.9 %shard_map.514 = (bf16[4096,128]{1,0:T(8,128)(2,1)}, bf16[4096,128]{1,0:T(8,128)(2,1)}) custom-call(bf16[2048,128]{1,0:T(8,128)(2,1)} %copy.107.packed, f32[4608,128]{1,0:T(8,128)} %get-tuple-element.45.ctx, bf16[2,4608,128]{2,1,0:T(8,128)(2,1)} %get-tuple-element.46.qa, bf16[4608,128]{1,0:T(8,128)(2,1)} %get-tuple-element.47.qw, ...), custom_call_target="tpu_custom_call" | custom-call | flops 49999998976 | bytes 20000000 | tf_op jit(solution)/shard_map/pallas_call | solution.py:389
  538.9 4.0 fusion.16
  544.8 4.9 convolution_add_fusion
  552.2 57.4 %reduce-scatter.10.cloned.1.call-done = f32[32,512]{1,0:T(8,128)} async-done(((f32[256,512]{1,0:T(8,128)}), f32[32,512]{1,0:T(8,128)}) %reduce-scatter.10.cloned.1.call-update) | async-done | bytes 65552 | tf_op jit(solution)/shard_map/reduce_scatter | solution.py:583
  612.3 19.5 %all-reduce.6 = (f32[2,64]{1,0:T(2,128)S(1)}, f32[512]{0:T(512)S(1)}) all-reduce(f32[2,64]{1,0:T(2,128)S(1)} %pad_maximum_fusion.1, f32[512]{0:T(512)S(1)} %get-tuple-element.249), channel_id=7, replica_groups=mesh['dp'=8,'tensor'=4] {'dp'}, use_global_device_ids=true, to_apply=%region_25.26.clone | all-reduce | flops 640 | bytes 5120
  633.1 39.9 %reduce-scatter.14.cloned.1.call-done = f32[32,6]{1,0:T(8,128)} async-done(((f32[256,6]{1,0:T(8,128)}), f32[32,6]{1,0:T(8,128)}) %reduce-scatter.14.cloned.1.call-update) | async-done | bytes 784
  674.4 62.7 %reduce-scatter.8.cloned.1.call-done = f32[64,32]{0,1:T(8,128)} async-done(((f32[64,256]{0,1:T(8,128)}), f32[64,32]{0,1:T(8,128)}) %reduce-scatter.8.cloned.1.call-update) | async-done | bytes 8208 | tf_op jit(solution)/shard_map/reduce_scatter | solution.py:582
  738.5 73.8 %all-reduce.21.cloned.1.call-done = f32[3,256,64]{2,0,1:T(4,128)} async-done(((f32[3,256,64]{2,0,1:T(4,128)}), f32[3,256,64]{2,0,1:T(4,128)}) %all-reduce.21.cloned.1.call-update) | async-done | bytes 196624
  813.8 85.6 %all-reduce.19.cloned.1.call-done = f32[4096,256]{1,0:T(8,128)} async-done(((f32[4096,256]{1,0:T(8,128)}), f32[4096,256]{1,0:T(8,128)}) %all-reduce.19.cloned.1.call-update) | async-done | bytes 4194320 | tf_op jit(solution)/shard_map/psum | solution.py:460
  899.4 6.0 add.234
  (172 shorter events, 43.3 us)
Async XLA Ops:
  7.2 242.4 %all-reduce.13.cloned.1.call-start = ((), (), s32[]{:S(2)}) async-start(), calls=%async_computation.4 | async-start | bytes 8388608 | tf_op jit(solution)/shard_map/psum | solution.py:460
  40.5 59.3 %copy-start.14 = (bf16[3,256,64]{2,1,0:T(8,128)(2,1)}, bf16[3,256,64]{2,1,0:T(8,128)(2,1)S(1)}, u32[]{:S(2)}) copy-start(bf16[3,256,64]{2,1,0:T(8,128)(2,1)S(1)} %all_gather.21) | copy-start | bytes 294916
  136.9 50.9 %copy-start.16 = (f32[512,32]{0,1:T(8,128)S(1)}, f32[512,32]{0,1:T(8,128)}, u32[]{:S(2)}) copy-start(f32[512,32]{0,1:T(8,128)} %param.34) | copy-start | bytes 196612
  137.0 112.6 %copy-start.4 = (bf16[4096,256]{1,0:T(8,128)(2,1)S(1)}, bf16[4096,256]{1,0:T(8,128)(2,1)}, u32[]{:S(2)}) copy-start(bf16[4096,256]{1,0:T(8,128)(2,1)} %tok.1) | copy-start | bytes 6291460
  139.8 226.2 %all-reduce.15.cloned.1.call-start = ((), (), s32[]{:S(2)}) async-start(), calls=%async_computation.5 | async-start | bytes 8388608 | tf_op jit(solution)/shard_map/psum | solution.py:460
  283.0 195.6 %all-reduce.17.cloned.1.call-start = ((), (), s32[]{:S(2)}) async-start(), calls=%async_computation.6 | async-start | bytes 8388608 | tf_op jit(solution)/shard_map/psum | solution.py:460
  392.8 157.2 %reduce-scatter.12.cloned.1.call-start = ((), (), s32[]{:S(2)}) async-start(), calls=%async_computation.10 | async-start | bytes 589824 | tf_op jit(solution)/shard_map/reduce_scatter | solution.py:584
  398.7 210.8 %reduce-scatter.10.cloned.1.call-start = ((), (), s32[]{:S(2)}) async-start(), calls=%async_computation.9 | async-start | bytes 589824 | tf_op jit(solution)/shard_map/reduce_scatter | solution.py:583
  405.0 268.0 %reduce-scatter.14.cloned.1.call-start = ((), (), s32[]{:S(2)}) async-start(), calls=%async_computation.11 | async-start | bytes 147456
  538.5 198.6 %reduce-scatter.8.cloned.1.call-start = ((), (), s32[]{:S(2)}) async-start(), calls=%async_computation.8 | async-start | bytes 147456 | tf_op jit(solution)/shard_map/reduce_scatter | solution.py:582
  542.8 269.4 %all-reduce.21.cloned.1.call-start = ((), (), s32[]{:S(2)}) async-start(), calls=%async_computation.12 | async-start | bytes 1048576
  544.8 354.7 %all-reduce.19.cloned.1.call-start = ((), (), s32[]{:S(2)}) async-start(), calls=%async_computation.7 | async-start | bytes 8388608 | tf_op jit(solution)/shard_map/psum | solution.py:460
  549.7 59.8 %copy-start.19 = (f32[32,512]{1,0:T(8,128)S(1)}, f32[32,512]{1,0:T(8,128)}, u32[]{:S(2)}) copy-start(f32[32,512]{1,0:T(8,128)} %param.33) | copy-start | bytes 196612
  549.7 59.8 %copy-start.23 = (f32[32,512]{1,0:T(8,128)S(1)}, f32[32,512]{1,0:T(8,128)}, u32[]{:S(2)}) copy-start(f32[32,512]{1,0:T(8,128)} %param.40) | copy-start | bytes 196612
  549.7 59.8 %copy-start.24 = (f32[32,512]{1,0:T(8,128)S(1)}, f32[32,512]{1,0:T(8,128)}, u32[]{:S(2)}) copy-start(f32[32,512]{1,0:T(8,128)} %param.47) | copy-start | bytes 196612
  549.8 61.3 %copy-start.9 = (bf16[4096,128]{1,0:T(8,128)(2,1)S(1)}, bf16[4096,128]{1,0:T(8,128)(2,1)}, u32[]{:S(2)}) copy-start(bf16[4096,128]{1,0:T(8,128)(2,1)} %get-tuple-element.52) | copy-start | bytes 3145732
  549.8 82.0 %copy-start.41 = (f32[64]{0:T(128)S(1)}, f32[64]{0:T(128)}, u32[]{:S(2)}) copy-start(f32[64]{0:T(128)} %param.37) | copy-start | bytes 772
  549.8 82.0 %copy-start.42 = (f32[64]{0:T(128)S(1)}, f32[64]{0:T(128)}, u32[]{:S(2)}) copy-start(f32[64]{0:T(128)} %param.44) | copy-start | bytes 772
  549.8 82.0 %copy-start.43 = (f32[64]{0:T(128)S(1)}, f32[64]{0:T(128)}, u32[]{:S(2)}) copy-start(f32[64]{0:T(128)} %param.51) | copy-start | bytes 772
  549.8 82.6 %copy-start.37 = (f32[2,8]{1,0:T(2,128)S(1)}, f32[2,8]{1,0:T(2,128)}, u32[]{:S(2)}) copy-start(f32[2,8]{1,0:T(2,128)} %param.36) | copy-start | bytes 196
  549.8 82.6 %copy-start.38 = (f32[2,8]{1,0:T(2,128)S(1)}, f32[2,8]{1,0:T(2,128)}, u32[]{:S(2)}) copy-start(f32[2,8]{1,0:T(2,128)} %param.43) | copy-start | bytes 196
  549.8 82.6 %copy-start.39 = (f32[2,8]{1,0:T(2,128)S(1)}, f32[2,8]{1,0:T(2,128)}, u32[]{:S(2)}) copy-start(f32[2,8]{1,0:T(2,128)} %param.50) | copy-start | bytes 196
  549.8 123.9 %copy-start.33 = (f32[6,32]{1,0:T(8,128)S(1)}, f32[6,32]{1,0:T(8,128)}, u32[]{:S(2)}) copy-start(f32[6,32]{1,0:T(8,128)} %param.35) | copy-start | bytes 2308
  549.9 123.9 %copy-start.34 = (f32[6,32]{1,0:T(8,128)S(1)}, f32[6,32]{1,0:T(8,128)}, u32[]{:S(2)}) copy-start(f32[6,32]{1,0:T(8,128)} %param.42) | copy-start | bytes 2308
  549.9 123.9 %copy-start.35 = (f32[6,32]{1,0:T(8,128)S(1)}, f32[6,32]{1,0:T(8,128)}, u32[]{:S(2)}) copy-start(f32[6,32]{1,0:T(8,128)} %param.49) | copy-start | bytes 2308
  549.9 187.2 %copy-start.26 = (f32[64,32]{0,1:T(8,128)S(1)}, f32[64,32]{0,1:T(8,128)}, u32[]{:S(2)}) copy-start(f32[64,32]{0,1:T(8,128)} %param.32) | copy-start | bytes 24580
  549.9 187.2 %copy-start.29 = (f32[64,32]{0,1:T(8,128)S(1)}, f32[64,32]{0,1:T(8,128)}, u32[]{:S(2)}) copy-start(f32[64,32]{0,1:T(8,128)} %param.39) | copy-start | bytes 24580
  549.9 187.2 %copy-start.30 = (f32[64,32]{0,1:T(8,128)S(1)}, f32[64,32]{0,1:T(8,128)}, u32[]{:S(2)}) copy-start(f32[64,32]{0,1:T(8,128)} %param.46) | copy-start | bytes 24580
  549.9 263.2 %copy-start.20 = (f32[3,32,64]{2,1,0:T(8,128)S(1)}, f32[3,32,64]{2,1,0:T(8,128)}, u32[]{:S(2)}) copy-start(f32[3,32,64]{2,1,0:T(8,128)} %param.31) | copy-start | bytes 73732
  549.9 263.2 %copy-start.27 = (f32[3,32,64]{2,1,0:T(8,128)S(1)}, f32[3,32,64]{2,1,0:T(8,128)}, u32[]{:S(2)}) copy-start(f32[3,32,64]{2,1,0:T(8,128)} %param.38) | copy-start | bytes 73732
  549.9 263.2 %copy-start.28 = (f32[3,32,64]{2,1,0:T(8,128)S(1)}, f32[3,32,64]{2,1,0:T(8,128)}, u32[]{:S(2)}) copy-start(f32[3,32,64]{2,1,0:T(8,128)} %param.45) | copy-start | bytes 73732
  673.8 231.7 %copy-start.31 = (f32[6,32]{1,0:T(8,128)}, f32[6,32]{1,0:T(8,128)S(1)}, u32[]{:S(2)}) copy-start(f32[6,32]{1,0:T(8,128)S(1)} %copy.113) | copy-start | bytes 2308
  (23 other events, 277.2 us)
Sparse Core Ops, SparseCore 0:
  139.9 86.8 all-reduce.12
  283.2 82.7 all-reduce.14
  392.9 85.6 all-reduce.16
  482.7 62.0 reduce-scatter.11
  548.6 60.8 reduce-scatter.9
  613.1 59.8 reduce-scatter.13
  677.2 59.8 reduce-scatter.7
  740.9 71.3 all-reduce.20
  814.6 84.7 all-reduce.18
